TPU v7x, 128 devices: a whole 4x4x4 slice. The times are simulated.
128 devices in a mesh: blk: 16 (over z_hi, x, core), head: 8 (over z_lo, y).
Axes of the slice: x: 4, y: 4, z: 4 (z_hi: 2, z_lo: 2; z = z_hi * 2 + z_lo), core: 2. Of those that a mesh axis runs over, the one named last changes fastest.
Arguments:
- tokens: bfloat16 [2, 8, 1024, 2048], P(None, 'head', 'blk'), may hold values from -6 to 6
- segment_ids: int32 [2, 8, 1024], replicated, may hold values from 0 to 1023, as said below
- ln1_gain: float32 [2048], replicated, may hold values from 0.5 to 1.5
- ln1_bias: float32 [2048], replicated, may hold values from -1 to 1
- w_query: bfloat16 [2048, 2048], P('blk', 'head'), may hold values from -0.125 to 0.125
- b_query: float32 [2048], replicated, may hold values from -1.5 to 1.5
- w_kv: bfloat16 [2048, 256], P('blk', 'head'), may hold values from -0.125 to 0.125
- b_value: float32 [128], replicated, may hold values from -2.5 to 2.5
- w_out: bfloat16 [2048, 2048], P('head', 'blk'), may hold values from -0.375 to 0.375
- b_out: float32 [2048], replicated, may hold values from -1.5 to 1.5
- ln2_gain: float32 [2048], replicated, may hold values from 0.5 to 1.5
- ln2_bias: float32 [2048], replicated, may hold values from -1 to 1
- w_fc: bfloat16 [2048, 8192], P('blk', 'head'), may hold values from -0.125 to 0.125
- b_fc: float32 [8192], replicated, may hold values from -1.5 to 1.5
- w_fc2: bfloat16 [8192, 2048], P('head', 'blk'), may hold values from -0.0625 to 0.0625
- b_fc2: float32 [2048], replicated, may hold values from -1.5 to 1.5
- cotangent: bfloat16 [2, 8, 1024, 2048], P(None, 'head', 'blk'), may hold values from -6 to 6
Outputs:
- output: bfloat16 [2, 8, 1024, 2048], P(None, 'head', 'blk')
- input_grad: float32 [2, 8, 1024, 2048], P(None, 'head', 'blk')
- ln1_gain_grad: float32 [2048], replicated
- ln1_bias_grad: float32 [2048], replicated
- w_query_grad: float32 [2048, 2048], P('blk', 'head')
- b_query_grad: float32 [2048], replicated
- w_kv_grad: float32 [2048, 256], P('blk', 'head')
- b_value_grad: float32 [128], replicated
- w_out_grad: float32 [2048, 2048], P('head', 'blk')
- b_out_grad: float32 [2048], replicated
- ln2_gain_grad: float32 [2048], replicated
- ln2_bias_grad: float32 [2048], replicated
- w_fc_grad: float32 [2048, 8192], P('blk', 'head')
- b_fc_grad: float32 [8192], replicated
- w_fc2_grad: float32 [8192, 2048], P('head', 'blk')
- b_fc2_grad: float32 [2048], replicated
Inputs may be any that keep to these rules, and one draw needn't show every extreme that they name: `segment_ids`: each position's id is the first position of its document within the sequence, so ids never fall along a sequence and position 0 has id 0; in every micro-batch some sequence is one single document, and some other sequence ends with a document of one position.
All inputs are finite; a program needn't handle non-finite values.
Results may differ from a plain program's by a relative error of at most 0.023.
Values may be sent and summed in bfloat16 or wider, within the bound.
No kernel may reach another device: no remote copies, remote signals or barrier semaphores. Data moves between devices by JAX's collectives and lax.ppermute only.
A program may use at most 192 MiB of HBM per device.

v0:
```python
import jax
import jax.numpy as jnp
from jax import lax
from jax.sharding import PartitionSpec as P

EPS = 1e-05
NEG = -1e30


def normalize(values, gain, shift):
    center = jnp.mean(values, axis=-1, keepdims=True)
    centered = values - center
    inv_std = lax.rsqrt(jnp.mean(centered * centered, axis=-1, keepdims=True) + EPS)
    normed = centered * inv_std
    return (normed * gain + shift, normed, inv_std)


def norm_back(grad, normed, inv_std, gain):
    scaled = grad * gain
    first_mean = jnp.mean(scaled, axis=-1, keepdims=True)
    second_mean = jnp.mean(scaled * normed, axis=-1, keepdims=True)
    return inv_std * (scaled - first_mean - normed * second_mean)


def gelu_tanh(values):
    return jax.nn.gelu(values, approximate=True)


def fetch_weights(w_query, w_kv, w_out, w_fc, w_fc2):
    return (
        lax.all_gather(w_query, "blk", axis=0, tiled=True),
        lax.all_gather(w_kv, "blk", axis=0, tiled=True),
        lax.all_gather(w_out, "blk", axis=1, tiled=True),
        lax.all_gather(w_fc, "blk", axis=0, tiled=True),
        lax.all_gather(w_fc2, "blk", axis=1, tiled=True),
    )


def settle_grads(grads):
    return (
        lax.psum_scatter(
            grads[0].astype(jnp.bfloat16), "blk", scatter_dimension=0, tiled=True
        ).astype(jnp.float32),
        lax.psum_scatter(
            grads[1].astype(jnp.bfloat16), "blk", scatter_dimension=0, tiled=True
        ).astype(jnp.float32),
        lax.psum_scatter(
            grads[2].astype(jnp.bfloat16), "blk", scatter_dimension=1, tiled=True
        ).astype(jnp.float32),
        lax.psum_scatter(
            grads[3].astype(jnp.bfloat16), "blk", scatter_dimension=0, tiled=True
        ).astype(jnp.float32),
        lax.psum_scatter(
            grads[4].astype(jnp.bfloat16), "blk", scatter_dimension=1, tiled=True
        ).astype(jnp.float32),
    )


def accumulate(running, fresh):
    if running is None:
        return fresh
    return jax.tree.map(lambda left, right: left + right, running, fresh)


def body(
    tokens,
    segment_ids,
    ln1_gain,
    ln1_bias,
    w_query,
    b_query,
    w_kv,
    b_value,
    w_out,
    b_out,
    ln2_gain,
    ln2_bias,
    w_fc,
    b_fc,
    w_fc2,
    b_fc2,
    cotangent,
):
    micro_count, seq_group, local_rows, model_width = tokens.shape
    head_dim = b_value.shape[0]
    hidden_total = b_fc.shape[0]
    n_head = lax.axis_size("head")
    n_blk = lax.axis_size("blk")
    head_id = lax.axis_index("head")
    blk_id = lax.axis_index("blk")
    seq_count = seq_group * n_head
    length = local_rows * n_blk
    q_cols = w_query.shape[1]
    heads_here = q_cols // head_dim
    kv_cols = w_kv.shape[1]
    hidden_here = w_fc.shape[1]
    score_scale = head_dim ** (-0.5)
    key_block = min(length, max(local_rows, 128))
    bias_query = lax.dynamic_slice_in_dim(b_query, head_id * q_cols, q_cols)
    kv_bias_full = jnp.concatenate([jnp.zeros((head_dim,), jnp.float32), b_value])
    bias_kv = lax.dynamic_slice_in_dim(kv_bias_full, head_id * kv_cols, kv_cols)
    bias_fc = lax.dynamic_slice_in_dim(b_fc, head_id * hidden_here, hidden_here)
    q_pos = blk_id * local_rows + jnp.arange(local_rows)
    own_rows = head_id * seq_group
    block_count = (blk_id * local_rows + local_rows - 1) // key_block + 1

    def own_part(values):
        return lax.dynamic_slice_in_dim(values, own_rows, seq_group, 0)

    results = []
    inputs_grads = []
    grad_total = None
    vector_total = None
    for mb_index in range(micro_count):
        batch_weights = fetch_weights(w_query, w_kv, w_out, w_fc, w_fc2)
        (
            query_weight_complete,
            key_value_weight_complete,
            output_weight_complete,
            up_weight_complete,
            down_weight_complete,
        ) = batch_weights
        seg_all = segment_ids[mb_index]
        q_seg = lax.dynamic_slice_in_dim(seg_all, blk_id * local_rows, local_rows, 1)
        x_all = lax.all_gather(tokens[mb_index], "head", axis=0, tiled=True)
        x_float = x_all.astype(jnp.float32)
        first_norm, first_normed, first_inv = normalize(x_float, ln1_gain, ln1_bias)
        normalized_reduced = first_norm.astype(jnp.bfloat16)
        queries = (
            jnp.einsum(
                "izj,jw->izw",
                normalized_reduced,
                query_weight_complete,
                preferred_element_type=jnp.float32,
            )
            + bias_query
        ).astype(jnp.bfloat16)
        queries = queries.reshape(seq_count, local_rows, heads_here, head_dim)
        kv_part = (
            jnp.einsum(
                "izj,jw->izw",
                normalized_reduced,
                key_value_weight_complete,
                preferred_element_type=jnp.float32,
            )
            + bias_kv
        ).astype(jnp.bfloat16)
        kv_here = lax.all_gather(kv_part, "head", axis=2, tiled=True)
        kv_all = lax.all_gather(kv_here, "blk", axis=1, tiled=True)

        def block_view(block_index):
            kv_piece = lax.dynamic_slice_in_dim(kv_all, block_index * key_block, key_block, 1)
            k_seg = lax.dynamic_slice_in_dim(seg_all, block_index * key_block, key_block, 1)
            k_pos = block_index * key_block + jnp.arange(key_block)
            allowed = (k_pos[None, None, :] <= q_pos[None, :, None]) & (
                k_seg[:, None, :] == q_seg[:, :, None]
            )
            scores = (
                jnp.einsum(
                    "slhe,ske->shlk",
                    queries,
                    kv_piece[..., :head_dim],
                    preferred_element_type=jnp.float32,
                )
                * score_scale
            )
            return (kv_piece, allowed[:, None], scores)

        def lse_step(block_index, carry):
            running_top, running_total = carry
            kv_piece, allowed, scores = block_view(block_index)
            masked = jnp.where(allowed, scores, NEG)
            new_top = jnp.maximum(running_top, jnp.max(masked, axis=-1))
            terms = jnp.where(allowed, jnp.exp(masked - new_top[..., None]), 0.0)
            running_total = running_total * jnp.exp(running_top - new_top) + jnp.sum(terms, axis=-1)
            return (new_top, running_total)

        init_state = (
            jnp.full((seq_count, heads_here, local_rows), NEG, jnp.float32),
            jnp.zeros((seq_count, heads_here, local_rows), jnp.float32),
        )
        final_top, final_total = lax.fori_loop(0, block_count, lse_step, init_state)
        log_total = final_top + jnp.log(final_total)

        def out_step(block_index, accumulated):
            kv_piece, allowed, scores = block_view(block_index)
            probs_low = jnp.where(allowed, jnp.exp(scores - log_total[..., None]), 0.0).astype(
                jnp.bfloat16
            )
            return accumulated + jnp.einsum(
                "shlk,ske->slhe",
                probs_low,
                kv_piece[..., head_dim:],
                preferred_element_type=jnp.float32,
            )

        attended = lax.fori_loop(
            0,
            block_count,
            out_step,
            jnp.zeros((seq_count, local_rows, heads_here, head_dim), jnp.float32),
        )
        attention_reduced = attended.astype(jnp.bfloat16).reshape(seq_count, local_rows, q_cols)
        projection_portion = jnp.einsum(
            "bjz,zf->bjf",
            attention_reduced,
            output_weight_complete,
            preferred_element_type=jnp.float32,
        )
        proj_total = lax.psum(projection_portion.astype(jnp.bfloat16), "head").astype(jnp.float32)
        residual = x_float + proj_total + b_out
        second_norm, second_normed_full, second_inv_full = normalize(residual, ln2_gain, ln2_bias)
        hidden_reduced = second_norm.astype(jnp.bfloat16)
        residual_own = own_part(residual)
        pre_act = (
            jnp.einsum(
                "apn,nk->apk",
                hidden_reduced,
                up_weight_complete,
                preferred_element_type=jnp.float32,
            )
            + bias_fc
        )
        activation_reduced = gelu_tanh(pre_act).astype(jnp.bfloat16)
        mlp_here = lax.psum_scatter(
            jnp.einsum(
                "umy,yz->umz",
                activation_reduced,
                down_weight_complete,
                preferred_element_type=jnp.float32,
            ).astype(jnp.bfloat16),
            "head",
            scatter_dimension=0,
            tiled=True,
        ).astype(jnp.float32)
        result = (residual_own + mlp_here + b_fc2).astype(jnp.bfloat16)
        grad_low = cotangent[mb_index]
        gradient_everything = lax.all_gather(grad_low, "head", axis=0, tiled=True)
        one_d_fc2 = jnp.einsum(
            "ktb,ktr->br",
            activation_reduced,
            gradient_everything,
            preferred_element_type=jnp.float32,
        )
        activation_gradient = jnp.einsum(
            "zui,yi->zuy",
            gradient_everything,
            down_weight_complete,
            preferred_element_type=jnp.float32,
        )
        _, gelu_pull = jax.vjp(gelu_tanh, pre_act)
        preactivation_gradient = gelu_pull(activation_gradient)[0].astype(jnp.bfloat16)
        one_d_fc = jnp.einsum(
            "avc,avr->cr",
            hidden_reduced,
            preactivation_gradient,
            preferred_element_type=jnp.float32,
        )
        g_fc_here = jnp.sum(preactivation_gradient.astype(jnp.float32), axis=(0, 1))
        d_hidden_part = jnp.einsum(
            "zrx,qx->zrq",
            preactivation_gradient,
            up_weight_complete,
            preferred_element_type=jnp.float32,
        )
        d_hidden = lax.psum(d_hidden_part.astype(jnp.bfloat16), "head").astype(jnp.float32)
        d_resid_full = gradient_everything.astype(jnp.float32) + norm_back(
            d_hidden, second_normed_full, second_inv_full, ln2_gain
        )
        residual_gradient_reduced = d_resid_full.astype(jnp.bfloat16)
        d_hidden_own = own_part(d_hidden)
        d_resid_own = own_part(d_resid_full)
        second_normed_own = own_part(second_normed_full)
        g_ln2_gain = jnp.sum(d_hidden_own * second_normed_own, axis=(0, 1))
        g_ln2_bias = jnp.sum(d_hidden_own, axis=(0, 1))
        g_b_out = jnp.sum(d_resid_own, axis=(0, 1))
        g_b_fc2 = jnp.sum(grad_low.astype(jnp.float32), axis=(0, 1))
        one_d_out = jnp.einsum(
            "uaz,uaw->zw",
            attention_reduced,
            residual_gradient_reduced,
            preferred_element_type=jnp.float32,
        )
        d_attn = jnp.einsum(
            "xma,wa->xmw",
            residual_gradient_reduced,
            output_weight_complete,
            preferred_element_type=jnp.float32,
        ).astype(jnp.bfloat16)
        d_attn = d_attn.reshape(seq_count, local_rows, heads_here, head_dim)
        delta = jnp.transpose(jnp.sum(d_attn.astype(jnp.float32) * attended, axis=-1), (0, 2, 1))

        def back_step(block_index, carry):
            d_query_acc, d_kv_acc = carry
            kv_piece, allowed, scores = block_view(block_index)
            probs = jnp.where(allowed, jnp.exp(scores - log_total[..., None]), 0.0)
            probs_low = probs.astype(jnp.bfloat16)
            d_probs = jnp.einsum(
                "slhe,ske->shlk",
                d_attn,
                kv_piece[..., head_dim:],
                preferred_element_type=jnp.float32,
            )
            d_scores = (probs * (d_probs - delta[..., None])).astype(jnp.bfloat16)
            d_query_acc = d_query_acc + jnp.einsum(
                "shlk,ske->slhe",
                d_scores,
                kv_piece[..., :head_dim],
                preferred_element_type=jnp.float32,
            )
            d_keys = (
                jnp.einsum("shlk,slhe->ske", d_scores, queries, preferred_element_type=jnp.float32)
                * score_scale
            )
            d_values = jnp.einsum(
                "shlk,slhe->ske", probs_low, d_attn, preferred_element_type=jnp.float32
            )
            d_kv_acc = lax.dynamic_update_slice_in_dim(
                d_kv_acc, jnp.concatenate([d_keys, d_values], axis=-1), block_index * key_block, 1
            )
            return (d_query_acc, d_kv_acc)

        back_init = (
            jnp.zeros((seq_count, local_rows, heads_here, head_dim), jnp.float32),
            jnp.zeros((seq_count, length, 2 * head_dim), jnp.float32),
        )
        d_query_acc, d_kv_acc = lax.fori_loop(0, block_count, back_step, back_init)
        query_gradient_reduced = (
            (d_query_acc * score_scale).astype(jnp.bfloat16).reshape(seq_count, local_rows, q_cols)
        )
        d_kv_block = lax.psum_scatter(
            d_kv_acc.astype(jnp.bfloat16), "blk", scatter_dimension=1, tiled=True
        )
        key_value_gradient_reduced = lax.psum_scatter(
            d_kv_block, "head", scatter_dimension=2, tiled=True
        )
        query_sums = jnp.sum(query_gradient_reduced.astype(jnp.float32), axis=(0, 1))
        g_b_query = lax.dynamic_update_slice_in_dim(
            jnp.zeros((model_width,), jnp.float32), query_sums, head_id * q_cols, 0
        )
        kv_sums = jnp.sum(key_value_gradient_reduced.astype(jnp.float32), axis=(0, 1))
        g_kv_full = lax.dynamic_update_slice_in_dim(
            jnp.zeros((2 * head_dim,), jnp.float32), kv_sums, head_id * kv_cols, 0
        )
        g_b_value = g_kv_full[head_dim:]
        g_b_fc = lax.dynamic_update_slice_in_dim(
            jnp.zeros((hidden_total,), jnp.float32), g_fc_here, head_id * hidden_here, 0
        )
        one_d_wq = jnp.einsum(
            "zpy,zpa->ya",
            normalized_reduced,
            query_gradient_reduced,
            preferred_element_type=jnp.float32,
        )
        one_d_wkv = jnp.einsum(
            "zpy,zpa->ya",
            normalized_reduced,
            key_value_gradient_reduced,
            preferred_element_type=jnp.float32,
        )
        d_norm_part = jnp.einsum(
            "hre,je->hrj",
            query_gradient_reduced,
            query_weight_complete,
            preferred_element_type=jnp.float32,
        ) + jnp.einsum(
            "hre,je->hrj",
            key_value_gradient_reduced,
            key_value_weight_complete,
            preferred_element_type=jnp.float32,
        )
        d_norm_here = lax.psum_scatter(
            d_norm_part.astype(jnp.bfloat16), "head", scatter_dimension=0, tiled=True
        ).astype(jnp.float32)
        normed_here = own_part(first_normed)
        d_input = d_resid_own + norm_back(d_norm_here, normed_here, own_part(first_inv), ln1_gain)
        g_ln1_gain = jnp.sum(d_norm_here * normed_here, axis=(0, 1))
        g_ln1_bias = jnp.sum(d_norm_here, axis=(0, 1))
        vectors = (
            g_ln1_gain,
            g_ln1_bias,
            g_b_query,
            g_b_value,
            g_b_out,
            g_ln2_gain,
            g_ln2_bias,
            g_b_fc,
            g_b_fc2,
        )
        result, d_input, grads, vectors = (
            result,
            d_input,
            (one_d_wq, one_d_wkv, one_d_out, one_d_fc, one_d_fc2),
            vectors,
        )
        results.append(result)
        inputs_grads.append(d_input)
        vector_total = accumulate(vector_total, vectors)
        grad_total = accumulate(grad_total, settle_grads(grads))
    summed = lax.psum(vector_total, ("blk", "head"))
    d_wq, d_wkv, d_out, d_fc, d_fc2 = grad_total
    return (
        jnp.stack(results),
        jnp.stack(inputs_grads),
        summed[0],
        summed[1],
        d_wq,
        summed[2],
        d_wkv,
        summed[3],
        d_out,
        summed[4],
        summed[5],
        summed[6],
        d_fc,
        summed[7],
        d_fc2,
        summed[8],
    )


def solution(mesh):
    return jax.shard_map(
        body,
        mesh=mesh,
        in_specs=(
            P(None, "head", "blk", None),
            P(),
            P(),
            P(),
            P("blk", "head"),
            P(),
            P("blk", "head"),
            P(),
            P("head", "blk"),
            P(),
            P(),
            P(),
            P("blk", "head"),
            P(),
            P("head", "blk"),
            P(),
            P(None, "head", "blk", None),
        ),
        out_specs=(
            P(None, "head", "blk", None),
            P(None, "head", "blk", None),
            P(),
            P(),
            P("blk", "head"),
            P(),
            P("blk", "head"),
            P(),
            P("head", "blk"),
            P(),
            P(),
            P(),
            P("blk", "head"),
            P(),
            P("head", "blk"),
            P(),
        ),
        check_vma=False,
    )
```

profile of v0, /device:TPU:1, one launch (start us, length us, event | category | flops | bytes accessed | tf_op | source)
XLA Modules:
  0.0 2153.1 jit_solution(1899038638080443421)
XLA Ops:
  150.6 53.2 %all-gather.25.cloned.1.call-done = bf16[8,1024,256]{2,0,1:T(8,128)(2,1)} async-done(((bf16[8,64,256]{2,0,1:T(8,128)(2,1)}), bf16[8,1024,256]{2,0,1:T(8,128)(2,1)}) %all-gather.25.cloned.1.call-update) | async-done | bytes 4194320 | tf_op jit(solution)/shard_map/all_gather | solution.py:149
  212.9 48.5 %all-gather.15.cloned.1.call-done = bf16[8,1024,256]{2,0,1:T(8,128)(2,1)} async-done(((bf16[8,64,256]{2,0,1:T(8,128)(2,1)}), bf16[8,1024,256]{2,0,1:T(8,128)(2,1)}) %all-gather.15.cloned.1.call-update) | async-done | bytes 4194320 | tf_op jit(solution)/shard_map/all_gather | solution.py:149
  270.7 36.9 %all-gather.19.cloned.1.call-done = bf16[256,2048]{1,0:T(8,128)(2,1)} async-done(((bf16[256,128]{1,0:T(8,128)(2,1)}), bf16[256,2048]{1,0:T(8,128)(2,1)}) %all-gather.19.cloned.1.call-update) | async-done | bytes 1048592 | tf_op jit(solution)/shard_map/all_gather | solution.py:33
  316.8 100.4 %all-reduce.12.cloned.1.call-done = (bf16[8,64,2048]{2,1,0:T(8,128)(2,1)}, bf16[8,64,2048]{2,1,0:T(8,128)(2,1)}) async-done(((bf16[8,64,2048]{2,1,0:T(8,128)(2,1)}, bf16[8,64,2048]{2,1,0:T(8,128)(2,1)}), (bf16[8,64,2048]{2,1,0:T(8,128)(2,1)}, bf16[8,64,2048]{2,1,0:T(8,128)(2,1)})) %all-reduce.12.cloned.1.call-update) | async-done | bytes 4194320 | tf_op jit(solution)/shard_map/psum | solution.py:210
  428.9 46.1 %all-gather.21.cloned.1.call-done = bf16[2048,1024]{1,0:T(8,128)(2,1)} async-done(((bf16[128,1024]{1,0:T(8,128)(2,1)}), bf16[2048,1024]{1,0:T(8,128)(2,1)}) %all-gather.21.cloned.1.call-update) | async-done | bytes 4194320 | tf_op jit(solution)/shard_map/all_gather | solution.py:34
  482.0 30.1 %all-gather.33.cloned.1.call-done = bf16[8,1,64,2048]{3,2,1,0:T(8,128)(2,1)} async-done(((bf16[1,1,64,2048]{3,2,1,0:T(8,128)(2,1)}), bf16[8,1,64,2048]{3,2,1,0:T(8,128)(2,1)}) %all-gather.33.cloned.1.call-update) | async-done | bytes 2097168 | tf_op jit(solution)/shard_map/all_gather | solution.py:238
  512.1 65.8 %all-gather.23.cloned.1.call-done = bf16[1024,2048]{1,0:T(8,128)(2,1)} async-done(((bf16[1024,128]{1,0:T(8,128)(2,1)}), bf16[1024,2048]{1,0:T(8,128)(2,1)}) %all-gather.23.cloned.1.call-update) | async-done | bytes 4194320 | tf_op jit(solution)/shard_map/all_gather | solution.py:35
  636.9 109.9 %all-reduce.10.cloned.1.call-done = (bf16[8,64,2048]{2,1,0:T(8,128)(2,1)}, bf16[8,64,2048]{2,1,0:T(8,128)(2,1)}) async-done(((bf16[8,64,2048]{2,1,0:T(8,128)(2,1)}, bf16[8,64,2048]{2,1,0:T(8,128)(2,1)}), (bf16[8,64,2048]{2,1,0:T(8,128)(2,1)}, bf16[8,64,2048]{2,1,0:T(8,128)(2,1)})) %all-reduce.10.cloned.1.call-update) | async-done | bytes 4194320 | tf_op jit(solution)/shard_map/psum | solution.py:266
  782.2 116.5 %reduce-scatter.41.cloned.1.call-done = bf16[8,64,256]{2,0,1:T(8,128)(2,1)} async-done(((bf16[8,1024,256]{2,0,1:T(8,128)(2,1)}), bf16[8,64,256]{2,0,1:T(8,128)(2,1)}) %reduce-scatter.41.cloned.1.call-update) | async-done | bytes 262160 | tf_op jit(solution)/shard_map/reduce_scatter | solution.py:331
  901.0 81.1 %reduce-scatter.35.cloned.1.call-done = bf16[8,64,256]{2,0,1:T(8,128)(2,1)} async-done(((bf16[8,1024,256]{2,0,1:T(8,128)(2,1)}), bf16[8,64,256]{2,0,1:T(8,128)(2,1)}) %reduce-scatter.35.cloned.1.call-update) | async-done | bytes 262160 | tf_op jit(solution)/shard_map/reduce_scatter | solution.py:331
  1100.6 43.6 %reduce-scatter.33.cloned.1.call-done = bf16[1,64,2048]{2,1,0:T(8,128)(2,1)} async-done(((bf16[8,64,2048]{2,1,0:T(8,128)(2,1)}), bf16[1,64,2048]{2,1,0:T(8,128)(2,1)}) %reduce-scatter.33.cloned.1.call-update) | async-done | bytes 262160 | tf_op jit(solution)/shard_map/reduce_scatter | solution.py:225
  1146.6 70.2 %reduce-scatter.61.cloned.1.call-done = bf16[128,256]{1,0:T(8,128)(2,1)} async-done(((bf16[2048,256]{1,0:T(8,128)(2,1)}), bf16[128,256]{1,0:T(8,128)(2,1)}) %reduce-scatter.61.cloned.1.call-update) | async-done | bytes 65552
  1217.7 69.0 %reduce-scatter.59.cloned.1.call-done = bf16[128,256]{1,0:T(8,128)(2,1)} async-done(((bf16[2048,256]{1,0:T(8,128)(2,1)}), bf16[128,256]{1,0:T(8,128)(2,1)}) %reduce-scatter.59.cloned.1.call-update) | async-done | bytes 65552
  1288.3 68.6 %reduce-scatter.49.cloned.1.call-done = bf16[128,256]{1,0:T(8,128)(2,1)} async-done(((bf16[2048,256]{1,0:T(8,128)(2,1)}), bf16[128,256]{1,0:T(8,128)(2,1)}) %reduce-scatter.49.cloned.1.call-update) | async-done | bytes 65552 | tf_op jit(solution)/shard_map/reduce_scatter | solution.py:41
  1356.9 70.0 %reduce-scatter.47.cloned.1.call-done = bf16[128,256]{1,0:T(8,128)(2,1)} async-done(((bf16[2048,256]{1,0:T(8,128)(2,1)}), bf16[128,256]{1,0:T(8,128)(2,1)}) %reduce-scatter.47.cloned.1.call-update) | async-done | bytes 65552 | tf_op jit(solution)/shard_map/reduce_scatter | solution.py:41
  1428.5 82.4 %reduce-scatter.65.cloned.1.call-done = bf16[128,1024]{1,0:T(8,128)(2,1)} async-done(((bf16[2048,1024]{1,0:T(8,128)(2,1)}), bf16[128,1024]{1,0:T(8,128)(2,1)}) %reduce-scatter.65.cloned.1.call-update) | async-done | bytes 262160
  1511.9 82.3 %reduce-scatter.63.cloned.1.call-done = bf16[128,1024]{1,0:T(8,128)(2,1)} async-done(((bf16[2048,1024]{1,0:T(8,128)(2,1)}), bf16[128,1024]{1,0:T(8,128)(2,1)}) %reduce-scatter.63.cloned.1.call-update) | async-done | bytes 262160
  1596.2 81.1 %reduce-scatter.53.cloned.1.call-done = bf16[128,1024]{1,0:T(8,128)(2,1)} async-done(((bf16[2048,1024]{1,0:T(8,128)(2,1)}), bf16[128,1024]{1,0:T(8,128)(2,1)}) %reduce-scatter.53.cloned.1.call-update) | async-done | bytes 262160 | tf_op jit(solution)/shard_map/reduce_scatter | solution.py:50
  1677.3 83.3 %reduce-scatter.51.cloned.1.call-done = bf16[128,1024]{1,0:T(8,128)(2,1)} async-done(((bf16[2048,1024]{1,0:T(8,128)(2,1)}), bf16[128,1024]{1,0:T(8,128)(2,1)}) %reduce-scatter.51.cloned.1.call-update) | async-done | bytes 262160 | tf_op jit(solution)/shard_map/reduce_scatter | solution.py:50
  1764.1 63.5 %reduce-scatter.57.cloned.1.call-done = bf16[128,32]{1,0:T(8,128)(2,1)} async-done(((bf16[2048,32]{1,0:T(8,128)(2,1)}), bf16[128,32]{1,0:T(8,128)(2,1)}) %reduce-scatter.57.cloned.1.call-update) | async-done | bytes 8208
  1828.4 67.8 %reduce-scatter.55.cloned.1.call-done = bf16[128,32]{1,0:T(8,128)(2,1)} async-done(((bf16[2048,32]{1,0:T(8,128)(2,1)}), bf16[128,32]{1,0:T(8,128)(2,1)}) %reduce-scatter.55.cloned.1.call-update) | async-done | bytes 8208
  1897.6 39.3 %reduce-scatter.39.cloned.1.call-done = bf16[1,64,2048]{2,1,0:T(8,128)(2,1)} async-done(((bf16[8,64,2048]{2,1,0:T(8,128)(2,1)}), bf16[1,64,2048]{2,1,0:T(8,128)(2,1)}) %reduce-scatter.39.cloned.1.call-update) | async-done | bytes 262160 | tf_op jit(solution)/shard_map/reduce_scatter | solution.py:372
  1938.4 42.1 %reduce-scatter.45.cloned.1.call-done = bf16[1,64,2048]{2,1,0:T(8,128)(2,1)} async-done(((bf16[8,64,2048]{2,1,0:T(8,128)(2,1)}), bf16[1,64,2048]{2,1,0:T(8,128)(2,1)}) %reduce-scatter.45.cloned.1.call-update) | async-done | bytes 262160 | tf_op jit(solution)/shard_map/reduce_scatter | solution.py:372
  1986.7 147.7 %all-reduce.8.cloned.1.call-done = (f32[2048]{0:T(1024)}, f32[2048]{0:T(1024)}, f32[2048]{0:T(1024)}, f32[128]{0:T(128)}, f32[2048]{0:T(1024)}, /*index=5*/f32[2...) async-done(((f32[2048]{0:T(1024)}, f32[2048]{0:T(1024)}, f32[2048]{0:T(1024)}, f32[128]{0:T(128)}, f32[2048]{0:T(1024)}, /*index=5*/f32[2048]{0:T(1024)}, ...) | async-done | bytes 90640 | tf_op jit(solution)/shard_map/psum | solution.py:400
  (391 shorter events, 458.5 us)
Async XLA Ops:
  10.6 193.2 %all-gather.25.cloned.1.call-start = ((), (), s32[]{:S(2)}) async-start(), calls=%async_computation.24 | async-start | bytes 4456448 | tf_op jit(solution)/shard_map/all_gather | solution.py:149
  82.0 179.4 %all-gather.15.cloned.1.call-start = ((), (), s32[]{:S(2)}) async-start(), calls=%async_computation.18 | async-start | bytes 4456448 | tf_op jit(solution)/shard_map/all_gather | solution.py:149
  124.4 183.3 %all-gather.19.cloned.1.call-start = ((), (), s32[]{:S(2)}) async-start(), calls=%async_computation.20 | async-start | bytes 1114112 | tf_op jit(solution)/shard_map/all_gather | solution.py:33
  124.9 292.3 %all-reduce.12.cloned.1.call-start = ((), (), s32[]{:S(2)}) async-start(), calls=%async_computation.48 | async-start | bytes 8388608 | tf_op jit(solution)/shard_map/psum | solution.py:210
  313.9 198.3 %all-gather.33.cloned.1.call-start = ((), (), s32[]{:S(2)}) async-start(), calls=%async_computation.39 | async-start | bytes 2359296 | tf_op jit(solution)/shard_map/all_gather | solution.py:238
  314.8 263.2 %all-gather.23.cloned.1.call-start = ((), (), s32[]{:S(2)}) async-start(), calls=%async_computation.22 | async-start | bytes 4456448 | tf_op jit(solution)/shard_map/all_gather | solution.py:35
  315.4 299.6 %all-gather.31.cloned.1.call-start = ((), (), s32[]{:S(2)}) async-start(), calls=%async_computation.38 | async-start | bytes 2359296 | tf_op jit(solution)/shard_map/all_gather | solution.py:238
  316.1 430.7 %all-reduce.10.cloned.1.call-start = ((), (), s32[]{:S(2)}) async-start(), calls=%async_computation.47 | async-start | bytes 8388608 | tf_op jit(solution)/shard_map/psum | solution.py:266
  636.9 261.8 %reduce-scatter.41.cloned.1.call-start = ((), (), s32[]{:S(2)}) async-start(), calls=%async_computation.29 | async-start | bytes 4456448 | tf_op jit(solution)/shard_map/reduce_scatter | solution.py:331
  773.4 208.7 %reduce-scatter.35.cloned.1.call-start = ((), (), s32[]{:S(2)}) async-start(), calls=%async_computation.26 | async-start | bytes 4456448 | tf_op jit(solution)/shard_map/reduce_scatter | solution.py:331
  782.1 280.1 %reduce-scatter.43.cloned.1.call-start = ((), (), s32[]{:S(2)}) async-start(), calls=%async_computation.30 | async-start | bytes 589824 | tf_op jit(solution)/shard_map/reduce_scatter | solution.py:334
  998.1 218.7 %reduce-scatter.61.cloned.1.call-start = ((), (), s32[]{:S(2)}) async-start(), calls=%async_computation.43 | async-start | bytes 1114112
  1002.4 284.2 %reduce-scatter.59.cloned.1.call-start = ((), (), s32[]{:S(2)}) async-start(), calls=%async_computation.42 | async-start | bytes 1114112
  1006.8 350.1 %reduce-scatter.49.cloned.1.call-start = ((), (), s32[]{:S(2)}) async-start(), calls=%async_computation.33 | async-start | bytes 1114112 | tf_op jit(solution)/shard_map/reduce_scatter | solution.py:41
  1012.6 414.3 %reduce-scatter.47.cloned.1.call-start = ((), (), s32[]{:S(2)}) async-start(), calls=%async_computation.32 | async-start | bytes 1114112 | tf_op jit(solution)/shard_map/reduce_scatter | solution.py:41
  1015.7 495.2 %reduce-scatter.65.cloned.1.call-start = ((), (), s32[]{:S(2)}) async-start(), calls=%async_computation.45 | async-start | bytes 4456448
  1029.1 565.1 %reduce-scatter.63.cloned.1.call-start = ((), (), s32[]{:S(2)}) async-start(), calls=%async_computation.44 | async-start | bytes 4456448
  1042.7 634.6 %reduce-scatter.53.cloned.1.call-start = ((), (), s32[]{:S(2)}) async-start(), calls=%async_computation.35 | async-start | bytes 4456448 | tf_op jit(solution)/shard_map/reduce_scatter | solution.py:50
  1050.5 710.1 %reduce-scatter.51.cloned.1.call-start = ((), (), s32[]{:S(2)}) async-start(), calls=%async_computation.34 | async-start | bytes 4456448 | tf_op jit(solution)/shard_map/reduce_scatter | solution.py:50
  1058.3 769.2 %reduce-scatter.57.cloned.1.call-start = ((), (), s32[]{:S(2)}) async-start(), calls=%async_computation.41 | async-start | bytes 557056
  1065.9 830.2 %reduce-scatter.55.cloned.1.call-start = ((), (), s32[]{:S(2)}) async-start(), calls=%async_computation.40 | async-start | bytes 557056
  1069.0 868.0 %reduce-scatter.39.cloned.1.call-start = ((), (), s32[]{:S(2)}) async-start(), calls=%async_computation.28 | async-start | bytes 2359296 | tf_op jit(solution)/shard_map/reduce_scatter | solution.py:372
  1073.4 907.1 %reduce-scatter.45.cloned.1.call-start = ((), (), s32[]{:S(2)}) async-start(), calls=%async_computation.31 | async-start | bytes 2359296 | tf_op jit(solution)/shard_map/reduce_scatter | solution.py:372
  1076.6 1057.9 %all-reduce.8.cloned.1.call-start = ((), (), s32[]{:S(2)}) async-start(), calls=%async_computation.46 | async-start | bytes 181248 | tf_op jit(solution)/shard_map/psum | solution.py:400
  (61 other events, 3554.7 us)
Sparse Core Ops, SparseCore 0:
  52.3 42.0 all-gather.26
  96.8 49.7 all-gather.16
  149.5 54.2 all-gather.24
  206.7 54.6 all-gather.14
  263.5 44.0 all-gather.18
  313.2 103.9 all-reduce.11
  419.6 55.2 all-gather.20
  514.2 63.6 all-gather.22
  637.0 109.7 all-reduce.9
  773.6 125.1 reduce-scatter.40
  903.2 78.8 reduce-scatter.34
  1059.3 41.2 reduce-scatter.30
  1102.8 41.3 reduce-scatter.32
  1148.0 68.6 reduce-scatter.60
  1220.9 65.7 reduce-scatter.58
  1291.1 65.7 reduce-scatter.48
  1361.2 65.6 reduce-scatter.46
  1431.0 79.7 reduce-scatter.64
  1515.3 78.8 reduce-scatter.62
  1598.3 78.9 reduce-scatter.52
  1681.7 78.8 reduce-scatter.50
  1764.2 63.3 reduce-scatter.56
  1831.8 64.3 reduce-scatter.54
  1988.0 146.4 all-reduce.7
  (7 shorter events, 257.9 us)
where the time goes:
time: 2160 us; the launch traced here: 2150 us
  waiting for transfers between devices  1780 us (82%)
  matrix products  139 us (6%)
  local copies, waits for them, and re-layouts  79.2 us (4%)
  blocking collectives  75.6 us (3%)
  other arithmetic  59.4 us (3%)
    unnamed x37, waiting for transfers between devices  439 us
    reduce_scatter x2, waiting for transfers between devices, body(): lax.psum_scatter(d_kv_acc.astype(jnp.bfloat16), 'blk', scatter_dimension=...  198 us
    reduce_scatter x2, waiting for transfers between devices, settle_grads(): lax.psum_scatter(grads[3].astype(jnp.bfloat16), 'blk', scatter_dimension=...  164 us
    psum x1, waiting for transfers between devices, body(): summed = lax.psum(vector_total, ('blk', 'head'))  148 us
    reduce_scatter x2, waiting for transfers between devices, settle_grads(): lax.psum_scatter(grads[0].astype(jnp.bfloat16), 'blk', scatter_dimension=...  139 us
    psum x1, waiting for transfers between devices, body(): lax.psum(d_hidden_part.astype(jnp.bfloat16), 'head').astype(jnp.float32)  110 us
    all_gather x2, waiting for transfers between devices, body(): kv_all = lax.all_gather(kv_here, 'blk', axis=1, tiled=True)  102 us
    psum x1, waiting for transfers between devices, body(): lax.psum(projection_portion.astype(jnp.bfloat16), 'head')  100 us
  transfers between devices with their start and end apart: 31, of which 29 were waited for; matrix products, arithmetic and copies ran while one was open for 9% of the time, Pallas kernels for 0%

commit v1 on v0

v1 whole, which is shorter than its diff:
```python
import functools

import jax
import jax.numpy as jnp
from jax import lax
from jax.experimental import pallas as pl
from jax.experimental.pallas import tpu as pltpu
from jax.sharding import Mesh
from jax.sharding import PartitionSpec as P

EPS = 1e-05
NEG = -1e30
F32 = jnp.float32
LOW = jnp.bfloat16
BLK = ("zh", "x", "c")
HEAD = ("zl", "y")
TEAM = ("c", "y")
PLANE = ("zh", "x", "zl")
LINE = ("zh", "x")
ALL = ("zh", "x", "c", "zl", "y")
Q_BLOCK = 256


def normalize(values, gain, shift):
    center = jnp.mean(values, axis=-1, keepdims=True)
    centered = values - center
    inv_std = lax.rsqrt(jnp.mean(centered * centered, axis=-1, keepdims=True) + EPS)
    normed = centered * inv_std
    return (normed * gain + shift, normed, inv_std)


def norm_back(grad, normed, inv_std, gain):
    scaled = grad * gain
    first_mean = jnp.mean(scaled, axis=-1, keepdims=True)
    second_mean = jnp.mean(scaled * normed, axis=-1, keepdims=True)
    return inv_std * (scaled - first_mean - normed * second_mean)


def gelu_tanh(values):
    return jax.nn.gelu(values, approximate=True)


def dot(left, right, left_dim, right_dim):
    return lax.dot_general(
        left, right, (((left_dim,), (right_dim,)), ((), ())), preferred_element_type=F32
    )


def block_probs(seg_ref, q_ref, keys, row, head, head_dim, scale):
    end = row + Q_BLOCK
    queries = q_ref[row:end, head * head_dim : (head + 1) * head_dim]
    scores = dot(queries, keys, 1, 1) * scale
    key_pos = lax.broadcasted_iota(jnp.int32, scores.shape, 1)
    query_pos = lax.broadcasted_iota(jnp.int32, scores.shape, 0) + row
    allowed = (key_pos <= query_pos) & (key_pos >= seg_ref[row:end, :])
    masked = jnp.where(allowed, scores, NEG)
    terms = jnp.exp(masked - jnp.max(masked, axis=1, keepdims=True))
    return queries, terms * (1.0 / jnp.sum(terms, axis=1, keepdims=True))


def attend_kernel(heads, head_dim, scale, seg_ref, qkv_ref, out_ref):
    wide = heads * head_dim
    for row in range(0, qkv_ref.shape[0], Q_BLOCK):
        end = row + Q_BLOCK
        keys = qkv_ref[:end, wide : wide + head_dim]
        values = qkv_ref[:end, wide + head_dim :]
        for head in range(heads):
            _, probs = block_probs(seg_ref, qkv_ref, keys, row, head, head_dim, scale)
            out_ref[row:end, head * head_dim : (head + 1) * head_dim] = dot(
                probs.astype(LOW), values, 1, 0
            ).astype(LOW)


def attend_back_kernel(heads, head_dim, scale, seg_ref, qkv_ref, grad_ref, out_ref, dkv_ref):
    wide = heads * head_dim
    dkv_ref[...] = jnp.zeros_like(dkv_ref)
    for row in range(0, qkv_ref.shape[0], Q_BLOCK):
        end = row + Q_BLOCK
        keys = qkv_ref[:end, wide : wide + head_dim]
        values = qkv_ref[:end, wide + head_dim :]
        for head in range(heads):
            cols = slice(head * head_dim, (head + 1) * head_dim)
            queries, probs = block_probs(seg_ref, qkv_ref, keys, row, head, head_dim, scale)
            grad = grad_ref[row:end, cols]
            d_probs = dot(grad, values, 1, 1)
            delta = jnp.sum(probs * d_probs, axis=1, keepdims=True)
            d_scores = (probs * (d_probs - delta)).astype(LOW)
            out_ref[row:end, cols] = (dot(d_scores, keys, 1, 0) * scale).astype(LOW)
            dkv_ref[:end, :head_dim] += dot(d_scores, queries, 0, 0)
            dkv_ref[:end, head_dim:] += dot(probs.astype(LOW), grad, 0, 0)
    out_ref[:, wide : wide + head_dim] = (dkv_ref[:, :head_dim] * scale).astype(LOW)
    out_ref[:, wide + head_dim :] = dkv_ref[:, head_dim:].astype(LOW)


def attend(segments, qkv, heads, head_dim):
    length = qkv.shape[0]
    return pl.pallas_call(
        functools.partial(attend_kernel, heads, head_dim, head_dim**-0.5),
        out_shape=jax.ShapeDtypeStruct((length, heads * head_dim), LOW),
        compiler_params=pltpu.CompilerParams(vmem_limit_bytes=40 * 2**20),
        cost_estimate=pl.CostEstimate(
            flops=2 * heads * length * length * head_dim,
            bytes_accessed=4 * qkv.size,
            transcendentals=heads * length * length // 2,
        ),
        name="attend",
    )(segments, qkv)


def attend_back(segments, qkv, grad, heads, head_dim):
    length = qkv.shape[0]
    return pl.pallas_call(
        functools.partial(attend_back_kernel, heads, head_dim, head_dim**-0.5),
        out_shape=jax.ShapeDtypeStruct(qkv.shape, LOW),
        scratch_shapes=[pltpu.VMEM((length, 2 * head_dim), F32)],
        compiler_params=pltpu.CompilerParams(vmem_limit_bytes=40 * 2**20),
        cost_estimate=pl.CostEstimate(
            flops=5 * heads * length * length * head_dim,
            bytes_accessed=8 * qkv.size,
            transcendentals=heads * length * length // 2,
        ),
        name="attend_back",
    )(segments, qkv, grad)


def team_gather(values):
    return lax.all_gather(values, TEAM, axis=0, tiled=True)


def team_scatter(partial):
    cores, ys = lax.axis_size("c"), lax.axis_size("y")
    rows = partial.shape[0] // (cores * ys)
    low = partial.astype(LOW).reshape(cores, ys, rows, partial.shape[1])
    core = lax.axis_index("c")
    kept = lax.dynamic_index_in_dim(low, core, 0, keepdims=False)
    sent = lax.dynamic_index_in_dim(low, 1 - core, 0, keepdims=False)
    got = lax.ppermute(sent, "c", [(0, 1), (1, 0)])
    both = (kept.astype(F32) + got.astype(F32)).astype(LOW)
    pieces = lax.all_to_all(both, "y", 0, 0, tiled=True)
    return jnp.sum(pieces.astype(F32), axis=0)


def swap(values):
    return lax.ppermute(values, ("c", "zl"), [(0, 0), (1, 2), (2, 1), (3, 3)])


def plane_gather(block):
    count = lax.axis_size(PLANE)
    spread = jnp.broadcast_to(block[None], (count,) + block.shape)
    whole = lax.all_to_all(spread, PLANE, 0, 0, tiled=True)
    return whole.reshape(count * block.shape[0], block.shape[1])


def plane_scatter(partial):
    count = lax.axis_size(PLANE)
    blocks = partial.astype(LOW).reshape(count, partial.shape[0] // count, partial.shape[1])
    return jnp.sum(lax.all_to_all(blocks, PLANE, 0, 0, tiled=True).astype(F32), axis=0)


def sum_vectors(flat):
    count = lax.axis_size(ALL)
    chunk = -(-flat.shape[0] // (count * 128)) * 128
    padded = jnp.pad(flat, (0, count * chunk - flat.shape[0])).reshape(count, chunk // 128, 128)
    mine = jnp.sum(lax.all_to_all(padded, ALL, 0, 0, tiled=True), axis=0)
    spread = jnp.broadcast_to(mine[None], padded.shape)
    return lax.all_to_all(spread, ALL, 0, 0, tiled=True).reshape(-1)[: flat.shape[0]]


def body(
    tokens,
    segment_ids,
    ln1_gain,
    ln1_bias,
    w_query,
    b_query,
    w_kv,
    b_value,
    w_out,
    b_out,
    ln2_gain,
    ln2_bias,
    w_fc,
    b_fc,
    w_fc2,
    b_fc2,
    cotangent,
):
    micro, _, rows, width = tokens.shape
    head_dim = b_value.shape[0]
    q_cols = w_query.shape[1]
    kv_cols = w_kv.shape[1]
    heads = q_cols // head_dim
    hidden = w_fc.shape[1]
    cores, ys = lax.axis_size("c"), lax.axis_size("y")
    lines = lax.axis_size(LINE)
    team_rank = lax.axis_index(TEAM)
    own = micro * rows

    def to_lines(values):
        cut = values.reshape(cores, ys, micro, rows, values.shape[-1])
        cut = jnp.transpose(cut, (2, 1, 0, 3, 4)).reshape(lines, cores * rows, values.shape[-1])
        moved = lax.all_to_all(cut, LINE, 0, 0, tiled=True)
        return moved.reshape(lines * cores * rows, values.shape[-1])

    def from_lines(values):
        cut = values.reshape(lines, cores * rows, values.shape[-1])
        moved = lax.all_to_all(cut, LINE, 0, 0, tiled=True)
        moved = moved.reshape(micro, ys, cores, rows, values.shape[-1])
        return jnp.transpose(moved, (2, 1, 0, 3, 4)).reshape(-1, values.shape[-1])

    early = swap(jnp.concatenate([w_query, w_kv], axis=1))
    kv_block = lax.all_gather(early[:, q_cols:], TEAM, axis=1, tiled=True)
    w_qkv = plane_gather(jnp.concatenate([early[:, :q_cols], kv_block], axis=1))
    late = swap(jnp.concatenate([w_out.T, w_fc, w_fc2.T], axis=1))
    w_out_t = plane_gather(late[:, :q_cols])
    w_up = plane_gather(late[:, q_cols : q_cols + hidden])
    w_down_t = plane_gather(late[:, q_cols + hidden :])

    x_own = tokens.reshape(own, width).astype(F32)
    first_norm, first_normed, first_inv = normalize(x_own, ln1_gain, ln1_bias)
    normed_in = team_gather(first_norm.astype(LOW))
    bias_qkv = jnp.concatenate(
        [
            lax.dynamic_slice_in_dim(b_query, team_rank * q_cols, q_cols),
            jnp.zeros((head_dim,), F32),
            b_value,
        ]
    )
    qkv = to_lines((dot(normed_in, w_qkv, 1, 0) + bias_qkv).astype(LOW))

    seq_rank = lax.axis_index("zl") * ys + lax.axis_index("x")
    segments = lax.dynamic_slice(
        segment_ids,
        (lax.axis_index("zh"), seq_rank, 0),
        (1, 1, segment_ids.shape[2]),
    ).reshape(-1, 1)
    attention = from_lines(attend(segments, qkv, heads, head_dim))

    projected = team_scatter(dot(attention, w_out_t, 1, 1))
    residual = x_own + projected + b_out
    second_norm, second_normed, second_inv = normalize(residual, ln2_gain, ln2_bias)
    hidden_in = team_gather(second_norm.astype(LOW))

    cot_own = cotangent.reshape(own, width)
    cot = team_gather(cot_own)
    pre_act = dot(hidden_in, w_up, 1, 0) + lax.dynamic_slice_in_dim(
        b_fc, team_rank * hidden, hidden
    )
    act, gelu_pull = jax.vjp(gelu_tanh, pre_act)
    act = act.astype(LOW)
    d_pre = gelu_pull(dot(cot, w_down_t, 1, 0))[0].astype(LOW)
    d_hidden = team_scatter(dot(d_pre, w_up, 1, 1))
    output = residual + team_scatter(dot(act, w_down_t, 1, 1)) + b_fc2
    output = output.astype(LOW).reshape(tokens.shape)
    g_down = plane_scatter(dot(cot, act, 0, 0))
    g_up = plane_scatter(dot(hidden_in, d_pre, 0, 0))

    cot_float = cot_own.astype(F32)
    d_res = cot_float + norm_back(d_hidden, second_normed, second_inv, ln2_gain)
    d_res_low = team_gather(d_res.astype(LOW))
    d_att = to_lines(dot(d_res_low, w_out_t, 1, 0).astype(LOW))
    g_out = plane_scatter(dot(d_res_low, attention, 0, 0))

    d_qkv = from_lines(attend_back(segments, qkv, d_att, heads, head_dim))
    d_in = team_scatter(dot(d_qkv, w_qkv, 1, 1))
    input_grad = d_res + norm_back(d_in, first_normed, first_inv, ln1_gain)
    g_qkv_part = dot(normed_in, d_qkv, 0, 0)
    g_qkv = plane_scatter(g_qkv_part)
    kv_pieces = lax.all_to_all(
        g_qkv[:, q_cols:].astype(LOW).reshape(-1, cores * ys, kv_cols),
        TEAM,
        1,
        1,
        tiled=True,
    )
    g_kv = jnp.sum(kv_pieces.astype(F32), axis=1)

    d_qkv_sums = jnp.sum(d_qkv.astype(F32), axis=0)
    w_qkv_float = w_qkv.astype(F32)
    ln1_bias_part = jnp.sum(w_qkv_float * d_qkv_sums, axis=1)
    ln1_gain_part = (jnp.sum(w_qkv_float * g_qkv_part, axis=1) - ln1_bias * ln1_bias_part) / ln1_gain
    placed_query = lax.dynamic_update_slice_in_dim(
        jnp.zeros(b_query.shape, F32), d_qkv_sums[:q_cols], team_rank * q_cols, 0
    )
    placed_fc = lax.dynamic_update_slice_in_dim(
        jnp.zeros(b_fc.shape, F32),
        jnp.sum(d_pre.astype(F32), axis=0),
        team_rank * hidden,
        0,
    )
    parts = [
        ln1_gain_part,
        ln1_bias_part,
        placed_query,
        d_qkv_sums[q_cols + head_dim :],
        jnp.sum(d_res, axis=0),
        jnp.sum(d_hidden * second_normed, axis=0),
        jnp.sum(d_hidden, axis=0),
        placed_fc,
        jnp.sum(cot_float, axis=0),
    ]
    summed = sum_vectors(jnp.concatenate(parts))
    vectors = []
    start = 0
    for part in parts:
        vectors.append(summed[start : start + part.shape[0]])
        start += part.shape[0]

    grads = swap(jnp.concatenate([g_qkv[:, :q_cols], g_kv, g_out, g_up, g_down], axis=1).astype(LOW))
    grads = grads.astype(F32)
    cuts = [0, q_cols, kv_cols, q_cols, hidden, hidden]
    edges = [sum(cuts[: i + 1]) for i in range(len(cuts))]
    d_wq, d_wkv, d_out, d_up, d_down = (
        grads[:, edges[i] : edges[i + 1]] for i in range(len(cuts) - 1)
    )
    return (
        output,
        input_grad.reshape(tokens.shape),
        vectors[0],
        vectors[1],
        d_wq,
        vectors[2],
        d_wkv,
        vectors[3],
        d_out.T,
        vectors[4],
        vectors[5],
        vectors[6],
        d_up,
        vectors[7],
        d_down.T,
        vectors[8],
    )


def solution(mesh):
    fine = Mesh(mesh.devices.reshape(2, 4, 2, 2, 4), ALL)
    activations = P(None, HEAD, BLK, None)
    rows_first, cols_first = P(BLK, HEAD), P(HEAD, BLK)
    return jax.shard_map(
        body,
        mesh=fine,
        in_specs=(
            activations,
            P(),
            P(),
            P(),
            rows_first,
            P(),
            rows_first,
            P(),
            cols_first,
            P(),
            P(),
            P(),
            rows_first,
            P(),
            cols_first,
            P(),
            activations,
        ),
        out_specs=(
            activations,
            activations,
            P(),
            P(),
            rows_first,
            P(),
            rows_first,
            P(),
            cols_first,
            P(),
            P(),
            P(),
            rows_first,
            P(),
            cols_first,
            P(),
        ),
        check_vma=False,
    )
```

time: 2160 us -> 760 us (0.35)
  waiting for transfers between devices: 1780 us -> 370 us
  starting transfers between devices: 1.65 us -> 100 us
  matrix products: 139 us -> 79.1 us
  local copies, waits for them, and re-layouts: 79.2 us -> 45.7 us
    reduce_scatter x12 -> x0, waiting for transfers between devices: 641 us -> none  [the longest x2 198 us: body(): lax.psum_scatter(d_kv_acc.astype(jnp.bfloat16), 'blk', scatter_dimension=...]
    unnamed x37 -> x4, waiting for transfers between devices: 439 us -> 0.73 us
    psum x3 -> x0, waiting for transfers between devices: 358 us -> none  [the longest x1 148 us: body(): summed = lax.psum(vector_total, ('blk', 'head'))]
    all_to_all x0 -> x17, waiting for transfers between devices: none -> 334 us  [the longest x4 147 us: plane_gather(): whole = lax.all_to_all(spread, PLANE, 0, 0, tiled=True)]
    all_gather x10 -> x4, waiting for transfers between devices: 344 us -> 13.3 us  [team_gather(): return lax.all_gather(values, TEAM, axis=0, tiled=True)]
    all_to_all x0 -> x17, starting transfers between devices: none -> 81.7 us  [the longest x4 20.9 us: plane_gather(): whole = lax.all_to_all(spread, PLANE, 0, 0, tiled=True)]
    dot_general x44 -> x12, matrix products: 139 us -> 79.1 us  [dot(): lax.dot_general(left, right, (((left_dim,), (right_dim,)), ((), ())), pre...]
    all_to_all x0 -> x2, blocking collectives: none -> 58.1 us  [team_scatter(): pieces = lax.all_to_all(both, 'y', 0, 0, tiled=True)]
  transfers between devices with their start and end apart: 31 -> 28, of which waited for: 29 -> 22; matrix products, arithmetic and copies ran while one was open for 9% -> 14% of each run, Pallas kernels for 0% -> 2%
where the time goes in v1:
time: 760 us; the launch traced here: 750 us
  waiting for transfers between devices  370 us (49%)
  starting transfers between devices  100 us (13%)
  blocking collectives  80.8 us (11%)
  matrix products  79.1 us (10%)
  other arithmetic  47 us (6%)
  local copies, waits for them, and re-layouts  45.7 us (6%)
  between operations  15 us (2%)
  Pallas kernels  13.1 us (2%)
    all_to_all x4, waiting for transfers between devices, plane_gather(): whole = lax.all_to_all(spread, PLANE, 0, 0, tiled=True)  147 us
    all_to_all x4, waiting for transfers between devices, plane_scatter(): lax.all_to_all(blocks, PLANE, 0, 0, tiled=True).astype(F32)  126 us
    dot_general x12, matrix products, dot(): lax.dot_general(left, right, (((left_dim,), (right_dim,)), ((), ())), pre...  79.1 us
    all_to_all x2, blocking collectives, team_scatter(): pieces = lax.all_to_all(both, 'y', 0, 0, tiled=True)  58.1 us
    all_gather x1, blocking collectives, body(): kv_block = lax.all_gather(early[:, q_cols:], TEAM, axis=1, tiled=True)  22.7 us
    all_to_all x4, starting transfers between devices, plane_gather(): whole = lax.all_to_all(spread, PLANE, 0, 0, tiled=True)  20.9 us
    all_to_all x4, starting transfers between devices, plane_scatter(): lax.all_to_all(blocks, PLANE, 0, 0, tiled=True).astype(F32)  17.2 us
    all_to_all x2, waiting for transfers between devices, from_lines(): moved = lax.all_to_all(cut, LINE, 0, 0, tiled=True)  17 us
  transfers between devices with their start and end apart: 28, of which 22 were waited for; matrix products, arithmetic and copies ran while one was open for 14% of the time, Pallas kernels for 2%

profile of v1, /device:TPU:1, one launch (start us, length us, event | category | flops | bytes accessed | tf_op | source)
XLA Modules:
  0.0 750.4 jit_solution(4879883430682254135)
XLA Ops:
  21.1 22.7 %all_gather.16 = bf16[128,256]{0,1:T(8,128)(2,1)S(1)} all-gather(bf16[128,32]{0,1:T(8,128)(2,1)S(1)} %slice.117), channel_id=1, replica_groups=mesh['zh'=2,'x'=4,'c'=2,'zl'=2,'y'=4] {'c','y'}, dimensions={1}, use_global_device_ids=true | all-gather | bytes 73728 | tf_op jit(solution)/shard_map/all_gather | solution.py:212
  45.5 7.9 %all-to-all-start = ((bf16[16,128,512]{2,1,0:T(8,128)(2,1)}), bf16[16,128,512]{2,1,0:T(8,128)(2,1)S(1)}, u32[]{:S(2)}, u32[]{:S(2)}) async-start(bf16[16,128,512]{2,1,0:T(8,128)(2,1)} %broadcast_in_dim.16), calls=%async_computation | async-start | bytes 4194304 | tf_op jit(solution)/shard_map/all_to_all | solution.py:150
  54.2 29.6 %all-to-all-done = bf16[16,128,512]{2,1,0:T(8,128)(2,1)S(1)} async-done(((bf16[16,128,512]{2,1,0:T(8,128)(2,1)}), bf16[16,128,512]{2,1,0:T(8,128)(2,1)S(1)}, u32[]{:S(2)}, u32[]{:S(2)}) %all-to-all-start) | async-done | bytes 2097184 | tf_op jit(solution)/shard_map/all_to_all | solution.py:150
  98.1 12.9 %all-to-all-done.1 = bf16[8,128,512]{2,1,0:T(8,128)(2,1)S(1)} async-done(((bf16[8,128,512]{2,1,0:T(8,128)(2,1)}), bf16[8,128,512]{2,1,0:T(8,128)(2,1)S(1)}, u32[]{:S(2)}, u32[]{:S(2)}) %all-to-all-start.1) | async-done | bytes 1048608 | tf_op jit(solution)/shard_map/all_to_all | solution.py:202
  119.9 11.5 %all-to-all-done.2 = bf16[8,128,256]{2,1,0:T(8,128)(2,1)S(1)} async-done(((bf16[8,128,256]{2,1,0:T(8,128)(2,1)}), bf16[8,128,256]{2,1,0:T(8,128)(2,1)S(1)}, u32[]{:S(2)}, u32[]{:S(2)}) %all-to-all-start.2) | async-done | bytes 524320 | tf_op jit(solution)/shard_map/all_to_all | solution.py:207
  137.4 15.4 %all-to-all-done.3 = bf16[16,128,256]{2,1,0:T(8,128)(2,1)S(1)} async-done(((bf16[16,128,256]{2,1,0:T(8,128)(2,1)}), bf16[16,128,256]{2,1,0:T(8,128)(2,1)S(1)}, u32[]{:S(2)}, u32[]{:S(2)}) %all-to-all-start.3) | async-done | bytes 1048608 | tf_op jit(solution)/shard_map/all_to_all | solution.py:150
  166.9 29.1 %all_to_all.95 = bf16[4,128,2048]{2,1,0:T(8,128)(2,1)S(1)} all-to-all(bf16[4,128,2048]{2,1,0:T(8,128)(2,1)S(1)} %fusion.10), channel_id=1, replica_groups=mesh['zh'=2,'x'=4,'c'=2,'zl'=2,'y'=4] {'y'}, dimensions={0} | all-to-all | bytes 4194304 | tf_op jit(solution)/shard_map/all_to_all | solution.py:139
  211.5 56.2 %all-to-all-done.5 = bf16[16,128,1024]{2,1,0:T(8,128)(2,1)} async-done(((bf16[16,128,1024]{2,1,0:T(8,128)(2,1)}), bf16[16,128,1024]{2,1,0:T(8,128)(2,1)}, u32[]{:S(2)}, u32[]{:S(2)}) %all-to-all-start.5) | async-done | bytes 4194336 | tf_op jit(solution)/shard_map/all_to_all | solution.py:150
  275.4 9.9 %fusion.42 = f32[1024,1024]{1,0:T(8,128)} fusion(bf16[1024,2048]{1,0:T(8,128)(2,1)} %all-gather.7.cloned.1.call-done, bf16[2048,1024]{1,0:T(8,128)(2,1)} %bitcast.18), kind=kOutput, calls=%fused_computation.114 | convolution fusion | flops 4294967296 | bytes 12582912 | tf_op jit(solution)/shard_map/dot_general | solution.py:44
  285.4 45.5 %all-to-all-done.6 = bf16[16,128,1024]{2,1,0:T(8,128)(2,1)} async-done(((bf16[16,128,1024]{2,1,0:T(8,128)(2,1)}), bf16[16,128,1024]{2,1,0:T(8,128)(2,1)}, u32[]{:S(2)}, u32[]{:S(2)}) %all-to-all-start.6) | async-done | bytes 4194336 | tf_op jit(solution)/shard_map/all_to_all | solution.py:150
  330.9 11.5 %convert_reduce_fusion.2 = (f32[1024]{0:T(1024)S(1)}, bf16[1024,1024]{1,0:T(8,128)(2,1)S(1)}) fusion(f32[1024,1024]{1,0:T(8,128)} %fusion.42, f32[1024]{0:T(1024)S(1)} %dynamic_slice.38, bf16[1024,2048]{1,0:T(8,128)(2,1)} %all-gather.9.cloned.1.call-done, bf16[2048,1024]{1,0:T(8,128)(2,1)} %bitcast.19), kind=kOutput, calls=%fused_computation.26 | convolution fusion | flops 4319083520 | bytes 14688256 | tf_op jit(solution)/shard_map/dot_general | solution.py:44
  356.5 29.1 %all_to_all.96 = bf16[4,128,2048]{2,1,0:T(8,128)(2,1)S(1)} all-to-all(bf16[4,128,2048]{2,1,0:T(8,128)(2,1)S(1)} %fusion.8), channel_id=1, replica_groups=mesh['zh'=2,'x'=4,'c'=2,'zl'=2,'y'=4] {'y'}, dimensions={0} | all-to-all | bytes 4194304 | tf_op jit(solution)/shard_map/all_to_all | solution.py:139
  389.8 8.4 %convolution_convert_fusion.4 = bf16[1024,2048]{1,0:T(8,128)(2,1)S(1)} fusion(bf16[2048,1024]{1,0:T(8,128)(2,1)} %bitcast.19, f32[1024,1024]{1,0:T(8,128)} %fusion.42, f32[1024]{0:T(1024)S(1)} %dynamic_slice.38), kind=kOutput, calls=%fused_computation.37 | convolution fusion | flops 4307550208 | bytes 12587008 | tf_op jit(solution)/shard_map/dot_general | solution.py:44
  410.1 13.3 %all-gather.11.cloned.1.call-done = bf16[1024,2048]{1,0:T(8,128)(2,1)} async-done(((bf16[128,2048]{1,0:T(8,128)(2,1)}), bf16[1024,2048]{1,0:T(8,128)(2,1)}) %all-gather.11.cloned.1.call-update) | async-done | bytes 4194320 | tf_op jit(solution)/shard_map/all_gather | solution.py:127
  427.7 12.8 %all-to-all-done.7 = bf16[4,128,2048]{2,1,0:T(8,128)(2,1)} async-done(((bf16[4,128,2048]{2,1,0:T(8,128)(2,1)}), bf16[4,128,2048]{2,1,0:T(8,128)(2,1)}, u32[]{:S(2)}, u32[]{:S(2)}) %all-to-all-start.7) | async-done | bytes 2097184 | tf_op jit(solution)/shard_map/all_to_all | solution.py:139
  447.3 9.4 %convolution_convert_fusion.2 = bf16[2048,1024]{1,0:T(8,128)(2,1)} fusion(bf16[1024,2048]{1,0:T(8,128)(2,1)} %all-gather.7.cloned.1.call-done, bf16[1024,1024]{1,0:T(8,128)(2,1)} %copy-done.33), kind=kOutput, calls=%fused_computation.35 | convolution fusion | flops 4297064448 | bytes 10485760 | tf_op jit(solution)/shard_map/dot_general | solution.py:44
  471.4 48.6 %all-to-all-done.17 = bf16[16,128,1024]{2,1,0:T(8,128)(2,1)} async-done(((bf16[16,128,1024]{2,1,0:T(8,128)(2,1)}), bf16[16,128,1024]{2,1,0:T(8,128)(2,1)}, u32[]{:S(2)}, u32[]{:S(2)}) %all-to-all-start.17) | async-done | bytes 4194336 | tf_op jit(solution)/shard_map/all_to_all | solution.py:157
  523.7 8.8 %convert_bitcast_fusion = bf16[128,16,8,128]{3,2,1,0:T(8,128)(2,1)S(1)} fusion(bf16[1024,2048]{1,0:T(8,128)(2,1)} %all-gather.9.cloned.1.call-done, f32[1024,1024]{1,0:T(8,128)} %fusion.42, f32[1024]{0:T(1024)S(1)} %dynamic_slice.38), kind=kOutput, calls=%fused_computation.25 | convolution fusion | flops 4307550208 | bytes 12587008 | tf_op jit(solution)/shard_map/dot_general | solution.py:44
  552.3 50.0 %all-to-all-done.18 = bf16[16,128,1024]{1,2,0:T(8,128)(2,1)} async-done(((bf16[16,128,1024]{1,2,0:T(8,128)(2,1)}), bf16[16,128,1024]{1,2,0:T(8,128)(2,1)}, u32[]{:S(2)}, u32[]{:S(2)}) %all-to-all-start.18) | async-done | bytes 4194336 | tf_op jit(solution)/shard_map/all_to_all | solution.py:157
  618.8 16.6 %all-to-all-done.14 = bf16[16,128,512]{2,1,0:T(8,128)(2,1)} async-done(((bf16[16,128,512]{2,1,0:T(8,128)(2,1)}), bf16[16,128,512]{2,1,0:T(8,128)(2,1)}, u32[]{:S(2)}, u32[]{:S(2)}) %all-to-all-start.14) | async-done | bytes 2097184 | tf_op jit(solution)/shard_map/all_to_all | solution.py:157
  642.1 11.0 %all-to-all-done.16 = bf16[16,128,256]{2,1,0:T(8,128)(2,1)S(1)} async-done(((bf16[16,128,256]{2,1,0:T(8,128)(2,1)}), bf16[16,128,256]{2,1,0:T(8,128)(2,1)S(1)}, u32[]{:S(2)}, u32[]{:S(2)}) %all-to-all-start.16) | async-done | bytes 1048608 | tf_op jit(solution)/shard_map/all_to_all | solution.py:157
  653.0 7.9 %all-to-all-start.15 = ((bf16[128,8,32]{0,2,1:T(8,128)(2,1)}), bf16[128,8,32]{0,2,1:T(8,128)(2,1)S(1)}, u32[]{:S(2)}, u32[]{:S(2)}) async-start(bf16[128,8,32]{0,2,1:T(8,128)(2,1)} %bitcast.48), calls=%async_computation.15 | async-start | bytes 131072 | tf_op jit(solution)/shard_map/all_to_all | solution.py:269
  718.3 7.9 %all-to-all-done.12 = f32[128,2,128]{2,1,0:T(2,128)S(1)} async-done(((f32[128,2,128]{2,1,0:T(2,128)}), f32[128,2,128]{2,1,0:T(2,128)S(1)}, u32[]{:S(2)}, u32[]{:S(2)}) %all-to-all-start.12) | async-done | bytes 131104 | tf_op jit(solution)/shard_map/all_to_all | solution.py:164
  732.9 8.2 %all-to-all-done.13 = f32[128,2,128]{2,1,0:T(2,128)S(1)} async-done(((f32[128,2,128]{2,1,0:T(2,128)}), f32[128,2,128]{2,1,0:T(2,128)S(1)}, u32[]{:S(2)}, u32[]{:S(2)}) %all-to-all-start.13) | async-done | bytes 131104 | tf_op jit(solution)/shard_map/all_to_all | solution.py:166
  (229 shorter events, 251.2 us)
Async XLA Ops:
  7.2 76.6 %all-gather.5.cloned.1.call-start = ((), (), s32[]{:S(2)}) async-start(), calls=%async_computation.19 | async-start | bytes 4718592 | tf_op jit(solution)/shard_map/all_gather | solution.py:127
  45.5 38.3 %all-to-all-start = ((bf16[16,128,512]{2,1,0:T(8,128)(2,1)}), bf16[16,128,512]{2,1,0:T(8,128)(2,1)S(1)}, u32[]{:S(2)}, u32[]{:S(2)}) async-start(bf16[16,128,512]{2,1,0:T(8,128)(2,1)} %broadcast_in_dim.16), calls=%async_computation | async-start | bytes 4194304 | tf_op jit(solution)/shard_map/all_to_all | solution.py:150
  90.2 20.8 %all-to-all-start.1 = ((bf16[8,128,512]{2,1,0:T(8,128)(2,1)}), bf16[8,128,512]{2,1,0:T(8,128)(2,1)S(1)}, u32[]{:S(2)}, u32[]{:S(2)}) async-start(bf16[8,128,512]{2,1,0:T(8,128)(2,1)} %bitcast.5), calls=%async_computation.1 | async-start | bytes 2097152 | tf_op jit(solution)/shard_map/all_to_all | solution.py:202
  94.0 25.7 %collective-permute-start.1 = (bf16[128,2304]{0,1:T(8,128)(2,1)S(1)}, bf16[128,2304]{0,1:T(8,128)(2,1)S(1)}, u32[]{:S(2)}, u32[]{:S(2)}) collective-permute-start(bf16[128,2304]{0,1:T(8,128)(2,1)S(1)} %pad_maximum_fusion), channel_id=1, source_target_pairs={{0,0},{4,8},{8,4},{12,12},{1,1},{5,9},{9,5},{13,13},{2,2},{6,10},{... | collective-permute-start | bytes 1769480 | tf_op jit(solution)/shard_map/ppermute | solution.py:144
  116.3 15.1 %all-to-all-start.2 = ((bf16[8,128,256]{2,1,0:T(8,128)(2,1)}), bf16[8,128,256]{2,1,0:T(8,128)(2,1)S(1)}, u32[]{:S(2)}, u32[]{:S(2)}) async-start(bf16[8,128,256]{2,1,0:T(8,128)(2,1)} %bitcast.7), calls=%async_computation.2 | async-start | bytes 1048576 | tf_op jit(solution)/shard_map/all_to_all | solution.py:207
  132.5 20.2 %all-to-all-start.3 = ((bf16[16,128,256]{2,1,0:T(8,128)(2,1)}), bf16[16,128,256]{2,1,0:T(8,128)(2,1)S(1)}, u32[]{:S(2)}, u32[]{:S(2)}) async-start(bf16[16,128,256]{2,1,0:T(8,128)(2,1)} %broadcast_in_dim.18), calls=%async_computation.3 | async-start | bytes 2097152 | tf_op jit(solution)/shard_map/all_to_all | solution.py:150
  136.2 139.2 %all-gather.7.cloned.1.call-start = ((), (), s32[]{:S(2)}) async-start(), calls=%async_computation.20 | async-start | bytes 4718592 | tf_op jit(solution)/shard_map/all_gather | solution.py:127
  205.9 61.8 %all-to-all-start.5 = ((bf16[16,128,1024]{2,1,0:T(8,128)(2,1)}), bf16[16,128,1024]{2,1,0:T(8,128)(2,1)}, u32[]{:S(2)}, u32[]{:S(2)}) async-start(bf16[16,128,1024]{2,1,0:T(8,128)(2,1)} %broadcast_in_dim.19), calls=%async_computation.5 | async-start | bytes 8388608 | tf_op jit(solution)/shard_map/all_to_all | solution.py:150
  210.6 120.3 %all-gather.9.cloned.1.call-start = ((), (), s32[]{:S(2)}) async-start(), calls=%async_computation.21 | async-start | bytes 4718592 | tf_op jit(solution)/shard_map/all_gather | solution.py:127
  270.1 60.7 %all-to-all-start.6 = ((bf16[16,128,1024]{2,1,0:T(8,128)(2,1)}), bf16[16,128,1024]{2,1,0:T(8,128)(2,1)}, u32[]{:S(2)}, u32[]{:S(2)}) async-start(bf16[16,128,1024]{2,1,0:T(8,128)(2,1)} %broadcast_in_dim.20), calls=%async_computation.6 | async-start | bytes 8388608 | tf_op jit(solution)/shard_map/all_to_all | solution.py:150
  274.7 148.8 %all-gather.11.cloned.1.call-start = ((), (), s32[]{:S(2)}) async-start(), calls=%async_computation.22 | async-start | bytes 4718592 | tf_op jit(solution)/shard_map/all_gather | solution.py:127
  405.6 34.9 %all-to-all-start.7 = ((bf16[4,128,2048]{2,1,0:T(8,128)(2,1)}), bf16[4,128,2048]{2,1,0:T(8,128)(2,1)}, u32[]{:S(2)}, u32[]{:S(2)}) async-start(bf16[4,128,2048]{2,1,0:T(8,128)(2,1)} %fusion.9), calls=%async_computation.7 | async-start | bytes 4194304 | tf_op jit(solution)/shard_map/all_to_all | solution.py:139
  440.5 18.5 %all-to-all-start.9 = ((bf16[8,128,256]{2,1,0:T(8,128)(2,1)}), bf16[8,128,256]{2,1,0:T(8,128)(2,1)S(1)}, u32[]{:S(2)}, u32[]{:S(2)}) async-start(bf16[8,128,256]{2,1,0:T(8,128)(2,1)} %bitcast.32), calls=%async_computation.9 | async-start | bytes 1048576 | tf_op jit(solution)/shard_map/all_to_all | solution.py:202
  459.0 61.0 %all-to-all-start.17 = ((bf16[16,128,1024]{2,1,0:T(8,128)(2,1)}), bf16[16,128,1024]{2,1,0:T(8,128)(2,1)}, u32[]{:S(2)}, u32[]{:S(2)}) async-start(bf16[16,128,1024]{2,1,0:T(8,128)(2,1)} %bitcast.173), calls=%async_computation.17 | async-start | bytes 8388608 | tf_op jit(solution)/shard_map/all_to_all | solution.py:157
  520.0 21.1 %all-to-all-start.10 = ((bf16[8,128,512]{2,1,0:T(8,128)(2,1)}), bf16[8,128,512]{2,1,0:T(8,128)(2,1)S(1)}, u32[]{:S(2)}, u32[]{:S(2)}) async-start(bf16[8,128,512]{2,1,0:T(8,128)(2,1)} %bitcast.34), calls=%async_computation.10 | async-start | bytes 2097152 | tf_op jit(solution)/shard_map/all_to_all | solution.py:207
  541.0 61.4 %all-to-all-start.18 = ((bf16[16,128,1024]{1,2,0:T(8,128)(2,1)}), bf16[16,128,1024]{1,2,0:T(8,128)(2,1)}, u32[]{:S(2)}, u32[]{:S(2)}) async-start(bf16[16,128,1024]{1,2,0:T(8,128)(2,1)} %bitcast.158), calls=%async_computation.18 | async-start | bytes 8388608 | tf_op jit(solution)/shard_map/all_to_all | solution.py:157
  602.4 33.0 %all-to-all-start.14 = ((bf16[16,128,512]{2,1,0:T(8,128)(2,1)}), bf16[16,128,512]{2,1,0:T(8,128)(2,1)}, u32[]{:S(2)}, u32[]{:S(2)}) async-start(bf16[16,128,512]{2,1,0:T(8,128)(2,1)} %bitcast.176), calls=%async_computation.14 | async-start | bytes 4194304 | tf_op jit(solution)/shard_map/all_to_all | solution.py:157
  614.4 46.5 %collective-permute-start.5 = (bf16[4,128,2048]{2,1,0:T(8,128)(2,1)}, bf16[4,128,2048]{2,1,0:T(8,128)(2,1)}, u32[]{:S(2)}, u32[]{:S(2)}) collective-permute-start(bf16[4,128,2048]{2,1,0:T(8,128)(2,1)} %dynamic-slice_bitcast_fusion), channel_id=1, source_target_pairs={{0,8},{8,0},{1,9},{9,1},{2,10},{10,2},{3,11},{11,3},{4,12},{12,4},... | collective-permute-start | bytes 6291464 | tf_op jit(solution)/shard_map/ppermute | solution.py:137
  635.4 17.7 %all-to-all-start.16 = ((bf16[16,128,256]{2,1,0:T(8,128)(2,1)}), bf16[16,128,256]{2,1,0:T(8,128)(2,1)S(1)}, u32[]{:S(2)}, u32[]{:S(2)}) async-start(bf16[16,128,256]{2,1,0:T(8,128)(2,1)} %bitcast.178), calls=%async_computation.16 | async-start | bytes 2097152 | tf_op jit(solution)/shard_map/all_to_all | solution.py:157
  653.0 12.8 %all-to-all-start.15 = ((bf16[128,8,32]{0,2,1:T(8,128)(2,1)}), bf16[128,8,32]{0,2,1:T(8,128)(2,1)S(1)}, u32[]{:S(2)}, u32[]{:S(2)}) async-start(bf16[128,8,32]{0,2,1:T(8,128)(2,1)} %bitcast.48), calls=%async_computation.15 | async-start | bytes 131072 | tf_op jit(solution)/shard_map/all_to_all | solution.py:269
  665.9 37.6 %all-to-all-start.11 = ((bf16[4,128,2048]{2,1,0:T(8,128)(2,1)}), bf16[4,128,2048]{2,1,0:T(8,128)(2,1)}, u32[]{:S(2)}, u32[]{:S(2)}) async-start(bf16[4,128,2048]{2,1,0:T(8,128)(2,1)} %fusion.7), calls=%async_computation.11 | async-start | bytes 4194304 | tf_op jit(solution)/shard_map/all_to_all | solution.py:139
  683.8 12.4 %collective-permute-start.6 = (bf16[128,2592]{0,1:T(8,128)(2,1)S(1)}, bf16[128,2592]{0,1:T(8,128)(2,1)S(1)}, u32[]{:S(2)}, u32[]{:S(2)}) collective-permute-start(bf16[128,2592]{0,1:T(8,128)(2,1)S(1)} %copy.154), channel_id=1, source_target_pairs={{0,0},{4,8},{8,4},{12,12},{1,1},{5,9},{9,5},{13,13},{2,2},{6,10},{... | collective-permute-start | bytes 1990664 | tf_op jit(solution)/shard_map/ppermute | solution.py:144
  711.5 14.6 %all-to-all-start.12 = ((f32[128,2,128]{2,1,0:T(2,128)}), f32[128,2,128]{2,1,0:T(2,128)S(1)}, u32[]{:S(2)}, u32[]{:S(2)}) async-start(f32[128,2,128]{2,1,0:T(2,128)} %bitcast.44), calls=%async_computation.12 | async-start | bytes 262144 | tf_op jit(solution)/shard_map/all_to_all | solution.py:164
  727.0 14.1 %all-to-all-start.13 = ((f32[128,2,128]{2,1,0:T(2,128)}), f32[128,2,128]{2,1,0:T(2,128)S(1)}, u32[]{:S(2)}, u32[]{:S(2)}) async-start(f32[128,2,128]{2,1,0:T(2,128)} %broadcast_in_dim.23), calls=%async_computation.13 | async-start | bytes 262144 | tf_op jit(solution)/shard_map/all_to_all | solution.py:166
  (38 other events, 475.4 us)
Sparse Core Ops, SparseCore 0:
  12.4 36.2 all-gather.4
  200.5 29.0 all-gather.6
  231.3 32.0 all-gather.8
  389.9 33.5 all-gather.10
